TPU v7x, 32 devices: a whole 2x2x4 slice. The times are simulated.
32 devices in a mesh: member: 2 (over core), space: 16 (over z, y, x).
Axes of the slice: x: 2, y: 2, z: 4, core: 2. Of those that a mesh axis runs over, the one named last changes fastest.
Arguments:
- background: bfloat16 [64, 256, 2560], P('member', 'space'), may hold values from -6 to 6
- obs_ens: bfloat16 [64, 20480], P('member', 'space'), may hold values from -6 to 6
- obs_value: bfloat16 [20480], P('space'), may hold values from -6 to 6
- obs_weight: bfloat16 [20480], P('space'), may hold values from 0.049804688 to 1
- obs_region: int32 [20480], P('space'), may hold values from 0 to 255, as said below
- region_order: int32 [256], replicated, may hold values from 0 to 255, each once
Outputs:
- analysis: bfloat16 [64, 256, 2560], P('member', 'space')
Inputs may be any that keep to these rules, and one draw needn't show every extreme that they name: `obs_region`: in each aligned block of 1280 entries (the observations of one index of space) no region is named more than 32 times, and the same region is named exactly 32 times in every block. `region_order`: each region once.
All inputs are finite; a program needn't handle non-finite values.
Results may differ from a plain program's by a relative error of at most 0.0043.
Values may be sent and summed in bfloat16 or wider, within the bound.
A program may use at most 128 MiB of HBM per device.

v0:
```python
import jax
import jax.numpy as jnp
from jax import lax
from jax.sharding import PartitionSpec as P

TRIAL_COUNT = 64
NS_ITERS = 4
CAP = 32


highest = lax.Precision.HIGHEST


def inverse_root(system):
    members = system.shape[-1]
    identity = jnp.eye(members, dtype=jnp.float32)
    frobenius = jnp.sqrt(jnp.sum(system * system, axis=(1, 2)))
    direct_root = system / frobenius[:, None, None]
    inverse_part = jnp.broadcast_to(identity, system.shape)
    for iteration in range(NS_ITERS):
        correction = 1.5 * identity - 0.5 * jnp.matmul(inverse_part, direct_root, precision=highest)
        direct_root = jnp.matmul(direct_root, correction, precision=highest)
        inverse_part = jnp.matmul(correction, inverse_part, precision=highest)
    return (inverse_part, frobenius)


def transform_weights(gram_block, projection):
    members = gram_block.shape[-1]
    identity = jnp.eye(members, dtype=jnp.float32)
    system = (members - 1.0) * identity + gram_block
    inverse_part, frobenius = inverse_root(system)
    inner = jnp.matmul(inverse_part, projection[:, :, None], precision=highest)
    mean_shift = jnp.matmul(inverse_part, inner, precision=highest)[:, :, 0] / frobenius[:, None]
    dispersion_factor = jnp.sqrt((members - 1.0) / frobenius)
    return dispersion_factor[:, None, None] * inverse_part + mean_shift[:, :, None]


def arrival_rank(region_hits):
    count_here, region_total = region_hits.shape
    block_rows = 128
    block_count = count_here // block_rows
    blocked = region_hits.reshape(block_count, block_rows, region_total)
    row_index = jnp.arange(block_rows, dtype=jnp.int32)
    earlier = (row_index[None, :] < row_index[:, None]).astype(jnp.bfloat16)
    within = jnp.einsum("ij,bjr->bir", earlier, blocked, preferred_element_type=jnp.float32)
    totals = jnp.sum(blocked.astype(jnp.float32), axis=1)
    offsets = jnp.cumsum(totals, axis=0) - totals
    counted = (within + offsets[:, None, :]) * blocked.astype(jnp.float32)
    return jnp.sum(counted, axis=2).reshape(count_here).astype(jnp.int32)


def shards(background, obs_ens, obs_value, obs_weight, obs_region, region_order):
    member_count = lax.axis_size("member")
    space_count = lax.axis_size("space")
    own_members, own_regions, model_variables = background.shape
    compute_regions = own_regions // member_count
    region_total = region_order.shape[0]
    device_total = member_count * space_count
    region_ids = jnp.arange(region_total, dtype=jnp.int32)
    position = jnp.sum(
        jnp.where(region_order[None, :] == region_ids[:, None], region_ids[None, :], 0), axis=1
    )
    region_match = obs_region[:, None] == region_ids[None, :]
    obs_pos = jnp.sum(jnp.where(region_match, position[None, :], 0), axis=1)
    arrival = arrival_rank(region_match.astype(jnp.bfloat16))
    owner_space = obs_pos // own_regions
    owner_member = obs_pos % own_regions // compute_regions
    local_slot = obs_pos % compute_regions
    target = (
        (owner_member * space_count + owner_space) * compute_regions + local_slot
    ) * CAP + arrival
    payload = jnp.concatenate([obs_ens, obs_weight[None, :], obs_value[None, :]], axis=0)
    device_slots = compute_regions * CAP
    group_devices = 8
    group_slots = group_devices * device_slots
    group_count = device_total // group_devices
    slot_index = jnp.arange(group_slots, dtype=jnp.int32)

    def fill_group(group):
        picks = (target[:, None] == group * group_slots + slot_index[None, :]).astype(jnp.bfloat16)
        return jnp.dot(payload, picks, preferred_element_type=jnp.float32).astype(jnp.bfloat16)

    filled = lax.map(fill_group, jnp.arange(group_count, dtype=jnp.int32))
    filled = jnp.moveaxis(filled, 1, 0).reshape(own_members + 2, device_total * device_slots)
    ens_send = filled[:own_members].reshape(own_members, member_count, space_count, device_slots)
    meta_send = filled[own_members:].reshape(2, member_count, space_count, device_slots)
    ens_flat, meta_flat = (
        lax.all_to_all(
            ens_send.reshape(own_members, device_total, device_slots),
            ("member", "space"),
            split_axis=1,
            concat_axis=1,
            tiled=True,
        ),
        lax.all_to_all(
            meta_send.reshape(2, device_total, device_slots),
            ("member", "space"),
            split_axis=1,
            concat_axis=1,
            tiled=True,
        ),
    )
    gathered_trials = ens_flat.reshape(own_members, member_count, space_count, device_slots)
    meta_recv = meta_flat.reshape(2, member_count, space_count, device_slots)
    background_trials = gathered_trials.astype(jnp.float32).reshape(
        own_members, member_count, space_count, compute_regions, CAP
    )
    meta_values = meta_recv[:, 0].astype(jnp.float32).reshape(2, space_count, compute_regions, CAP)
    measured_average = jnp.sum(background_trials, axis=(0, 1)) / TRIAL_COUNT
    trial_perturbation = background_trials - measured_average[None, None]
    departure = meta_values[1] - measured_average
    weighted = trial_perturbation * meta_values[0][None, None]
    gram_block = jnp.einsum(
        "kmscq,jnscq->cmknj", weighted, trial_perturbation, precision=highest
    ).reshape(compute_regions, TRIAL_COUNT, TRIAL_COUNT)
    projection = jnp.einsum("kmscq,scq->cmk", weighted, departure, precision=highest).reshape(
        compute_regions, TRIAL_COUNT
    )
    weights = transform_weights(gram_block, projection).astype(jnp.bfloat16)
    all_weights = lax.all_gather(weights, "member", axis=0, tiled=True)
    member_position_index = lax.axis_index("member")
    own_columns = lax.dynamic_slice_in_dim(
        all_weights, member_position_index * own_members, own_members, 2
    )
    state_block = lax.all_gather(background, "member", axis=0, tiled=True)
    combined = jnp.einsum(
        "ipf,pij->jpf", state_block, own_columns, preferred_element_type=jnp.float32
    )
    state_sum = jnp.sum(state_block.astype(jnp.float32), axis=0)
    combined, state_sum = (combined, state_sum)
    retained_fraction = 1.0 - jnp.sum(own_columns.astype(jnp.float32), axis=1)
    analysis = (
        combined + (state_sum / TRIAL_COUNT)[None] * retained_fraction.T[:, :, None]
    ).astype(jnp.bfloat16)
    return analysis


def solution(mesh):
    return jax.shard_map(
        shards,
        mesh=mesh,
        in_specs=(
            P("member", "space", None),
            P("member", "space"),
            P("space"),
            P("space"),
            P("space"),
            P(),
        ),
        out_specs=P("member", "space", None),
        check_vma=False,
    )
```

profile of v0, /device:TPU:0, one launch (start us, length us, event | category | flops | bytes accessed | tf_op | source)
XLA Modules:
  0.0 109.9 jit_solution(12842819725256560075)
XLA Ops:
  6.5 1.0 convert_reduce_fusion.1
  7.5 1.3 %fusion.21 = f32[10,128]{1,0:T(8,128)S(1)} fusion(f32[10,256]{1,0:T(8,128)S(1)} %sub.72, s32[10,128]{1,0:T(8,128)} %bitcast.90), kind=kOutput, calls=%fused_computation.26 | convolution fusion | flops 86194944 | bytes 20480 | tf_op jit(solution)/shard_map/ij,bjr->bir/dot_general | solution.py:45
  8.8 0.8 select_reduce_fusion.1
  9.6 1.1 %select_reduce_fusion = s32[1280]{0:T(1024)S(1)} fusion(s32[256]{0:T(256)S(1)} %select_reduce_fusion.1, s32[1280]{0:T(1024)} %param.12), kind=kLoop, calls=%fused_computation.24 | loop fusion | flops 981760 | bytes 11264 | tf_op jit(solution)/shard_map/reduce_sum | solution.py:64
  10.8 0.7 broadcast_in_dim.45
  11.4 0.7 broadcast_in_dim.46
  12.2 0.9 pad_maximum_fusion
  13.1 13.0 %while.11 = (s32[]{:T(128)}, bf16[4,34,2048]{2,1,0:T(8,128)(2,1)S(1)}, s32[1280]{0:T(1024)S(1)}, s32[4]{0:T(128)S(1)}, bf16[34,1280]{1,0:T(8,128)(2,1)S(1)}, /*index=5*/s32[]{:T(128)}, s32[1]{0:T(128)}) while((s32[]{:T(128)}, bf16[4,34,2048]{2,1,0:T(8,128)(2,1)S(1)}, s32[1280]{0:T(1024)S(1)}, s32[4]{0:T(128)S(1)}, ...), condition=%wide.region_6.7_spmd.clone, body=%wide.region_5.6_spmd.clone.sunk | while | flops 180951040 | bytes 290925 | solution.py:83
  13.1 0.7 dynamic_slice.11
  14.6 1.8 %fusion.89 = bf16[4,34,2048]{2,1,0:T(8,128)(2,1)S(1)} fusion(bf16[4,34,2048]{2,1,0:T(8,128)(2,1)S(1)} %get-tuple-element.111, s32[]{:T(128)} %get-tuple-element.110, bf16[34,1280]{1,0:T(8,128)(2,1)S(1)} %get-tuple-element.121, s32[2048]{0:T(1024)S(1)} %iota_add_fusion.2, s32[1280]{0:T(1024)S(1)} %get-tuple-element.119), kind=kOutput, calls=%fused_computation.7.clone.1 | convolution fusion | flops 180948992 | bytes 282628 | tf_op jit(solution)/shard_map/while/body/eval_jaxpr/dot_general | solution.py:81
  16.4 0.7 dynamic_slice.11
  17.8 1.8 %fusion.89 = bf16[4,34,2048]{2,1,0:T(8,128)(2,1)S(1)} fusion(bf16[4,34,2048]{2,1,0:T(8,128)(2,1)S(1)} %get-tuple-element.111, s32[]{:T(128)} %get-tuple-element.110, bf16[34,1280]{1,0:T(8,128)(2,1)S(1)} %get-tuple-element.121, s32[2048]{0:T(1024)S(1)} %iota_add_fusion.2, s32[1280]{0:T(1024)S(1)} %get-tuple-element.119), kind=kOutput, calls=%fused_computation.7.clone.1 | convolution fusion | flops 180948992 | bytes 282628 | tf_op jit(solution)/shard_map/while/body/eval_jaxpr/dot_general | solution.py:81
  19.7 0.7 dynamic_slice.11
  21.0 1.8 %fusion.89 = bf16[4,34,2048]{2,1,0:T(8,128)(2,1)S(1)} fusion(bf16[4,34,2048]{2,1,0:T(8,128)(2,1)S(1)} %get-tuple-element.111, s32[]{:T(128)} %get-tuple-element.110, bf16[34,1280]{1,0:T(8,128)(2,1)S(1)} %get-tuple-element.121, s32[2048]{0:T(1024)S(1)} %iota_add_fusion.2, s32[1280]{0:T(1024)S(1)} %get-tuple-element.119), kind=kOutput, calls=%fused_computation.7.clone.1 | convolution fusion | flops 180948992 | bytes 282628 | tf_op jit(solution)/shard_map/while/body/eval_jaxpr/dot_general | solution.py:81
  22.9 0.7 dynamic_slice.11
  24.3 1.8 %fusion.89 = bf16[4,34,2048]{2,1,0:T(8,128)(2,1)S(1)} fusion(bf16[4,34,2048]{2,1,0:T(8,128)(2,1)S(1)} %get-tuple-element.111, s32[]{:T(128)} %get-tuple-element.110, bf16[34,1280]{1,0:T(8,128)(2,1)S(1)} %get-tuple-element.121, s32[2048]{0:T(1024)S(1)} %iota_add_fusion.2, s32[1280]{0:T(1024)S(1)} %get-tuple-element.119), kind=kOutput, calls=%fused_computation.7.clone.1 | convolution fusion | flops 180948992 | bytes 282628 | tf_op jit(solution)/shard_map/while/body/eval_jaxpr/dot_general | solution.py:81
  26.1 0.6 slice.27
  26.7 7.3 %all-to-all-start.1 = ((bf16[2,32,256]{2,0,1:T(2,128)(2,1)}), bf16[2,32,256]{2,0,1:T(2,128)(2,1)S(1)}, u32[]{:S(2)}, u32[]{:S(2)}) async-start(bf16[2,32,256]{2,0,1:T(2,128)(2,1)} %bitcast.8), calls=%async_computation.1 | async-start | bytes 65536 | tf_op jit(solution)/shard_map/all_to_all | solution.py:95
  34.1 2.9 %copy.40 = bf16[32,16,2560]{2,0,1:T(8,128)(2,1)} copy(bf16[32,16,2560]{2,1,0:T(8,128)(2,1)S(1)} %copy-done.1) | data formatting | bytes 5242880 | tf_op args[0]
  37.1 0.4 copy.30
  37.5 0.4 reshape_reshape.6
  37.9 1.1 copy.31
  39.0 2.3 %all-to-all-done.1 = bf16[2,32,256]{2,0,1:T(2,128)(2,1)S(1)} async-done(((bf16[2,32,256]{2,0,1:T(2,128)(2,1)}), bf16[2,32,256]{2,0,1:T(2,128)(2,1)S(1)}, u32[]{:S(2)}, u32[]{:S(2)}) %all-to-all-start.1) | async-done | bytes 32800 | tf_op jit(solution)/shard_map/all_to_all | solution.py:95
  41.2 3.6 %all-to-all-start = ((bf16[32,32,256]{2,0,1:T(8,128)(2,1)}), bf16[32,32,256]{2,0,1:T(8,128)(2,1)S(1)}, u32[]{:S(2)}, u32[]{:S(2)}) async-start(bf16[32,32,256]{2,0,1:T(8,128)(2,1)} %copy.31), calls=%async_computation | async-start | bytes 1048576 | tf_op jit(solution)/shard_map/all_to_all | solution.py:88
  45.1 16.5 %all-to-all-done = bf16[32,32,256]{2,0,1:T(8,128)(2,1)S(1)} async-done(((bf16[32,32,256]{2,0,1:T(8,128)(2,1)}), bf16[32,32,256]{2,0,1:T(8,128)(2,1)S(1)}, u32[]{:S(2)}, u32[]{:S(2)}) %all-to-all-start) | async-done | bytes 524320 | tf_op jit(solution)/shard_map/all_to_all | solution.py:88
  61.9 0.3 copy.32
  62.2 2.5 %reshape.120 = f32[32,2,16,8,32]{4,3,2,1,0:T(8,128)} reshape(f32[32,32,256]{2,1,0:T(8,128)S(1)} %copy.32) | data formatting | bytes 2097152 | tf_op jit(solution)/shard_map/convert_element_type | solution.py:105
  64.7 3.5 %subtract_bitcast_fusion = (f32[32,2,16,8,32,1]{4,3,2,1,0,5:T(8,128)S(1)}, f32[32,2,16,8,32,1]{4,3,2,1,0,5:T(8,128)S(1)}) fusion(f32[32,2,16,8,32]{4,3,2,1,0:T(8,128)} %reshape.120, f32[16,8,32]{2,1,0:T(8,128)S(1)} %get-tuple-element.63, f32[16,8,32]{2,1,0:T(8,128)S(1)} %mul.102), kind=kLoop, calls=%fused_computation.17 | loop fusion | flops 524288 | bytes 3178496 | tf_op jit(solution)/shard_map/sub | solution.py:110
  68.2 15.0 %multiply_reduce_fusion.1 = (f32[8]{0:T(128)S(1)}, f32[8,2,32,2,32]{2,4,1,3,0:T(8,128)S(1)}) fusion(f32[2,32,2,32]{1,3,0,2:T(8,128)S(1)} %compare_select_fusion, f32[32,2,16,8,32,1]{4,3,2,1,0,5:T(8,128)S(1)} %get-tuple-element.61, f32[32,2,16,8,32,1]{4,3,2,1,0,5:T(8,128)S(1)} %get-tuple-element.60), kind=kOutput, calls=%fused_computation.38 | convolution fusion | flops 201424896 | bytes 2244640 | tf_op jit(solution)/shard_map/kmscq,jnscq->cmknj/dot_general | solution.py:113
  83.8 3.0 %multiply_reduce_fusion = f32[8,32,2]{0,2,1:T(2,128)S(1)} fusion(f32[32,2,16,8,32]{4,3,2,1,0:T(8,128)} %reshape.120, f32[8,32,16]{1,0,2:T(8,128)S(1)} %get-tuple-element.62, f32[16,8,32]{2,1,0:T(8,128)S(1)} %mul.102, f32[16,8,32]{2,1,0:T(8,128)S(1)} %get-tuple-element.63), kind=kLoop, calls=%fused_computation.15 | loop fusion | flops 1048064 | bytes 1099776
  87.0 0.5 fusion.30
  87.4 0.4 fusion.32
  87.8 0.4 fusion.40
  88.2 0.4 fusion.29
  88.6 0.4 fusion.54
  89.0 0.4 fusion.53
  89.4 0.4 fusion.28
  89.8 0.4 fusion.56
  90.2 0.4 fusion.55
  90.6 0.4 fusion.27
  91.0 0.4 fusion.57
  91.4 0.5 convolution_bitcast_fusion
  91.9 0.5 fusion.58
  92.7 2.0 %all_gather.6 = bf16[16,64,64]{2,1,0:T(8,128)(2,1)S(1)} all-gather(bf16[8,64,64]{2,1,0:T(8,128)(2,1)S(1)} %add_convert_fusion), channel_id=1, replica_groups=mesh['member'=2,'space'=16] {'member'}, dimensions={0}, use_global_device_ids=true | all-gather | bytes 196608 | tf_op jit(solution)/shard_map/all_gather | solution.py:120
  95.2 3.6 %convert_reduce_fusion = f32[16,2560]{1,0:T(8,128)S(1)} fusion(bf16[64,16,2560]{2,0,1:T(8,128)(2,1)} %all-gather.2.cloned.1.call-done), kind=kLoop, calls=%fused_computation.9 | loop fusion | flops 5201920 | bytes 5406720 | tf_op jit(solution)/shard_map/reduce_sum | solution.py:129
  98.8 0.4 copy-done
  99.2 0.9 fusion.15
  100.2 2.9 %copy.41 = bf16[32,16,2560]{2,1,0:T(8,128)(2,1)} copy(bf16[32,16,2560]{2,0,1:T(8,128)(2,1)S(1)} %fusion.15) | data formatting | bytes 5242880 | tf_op jit(solution)/shard_map/convert_element_type | solution.py:134
  (41 shorter events, 2.1 us)
Async XLA Ops:
  13.1 21.0 %copy-start.1 = (bf16[32,16,2560]{2,1,0:T(8,128)(2,1)S(1)}, bf16[32,16,2560]{2,1,0:T(8,128)(2,1)}, u32[]{:S(2)}) copy-start(bf16[32,16,2560]{2,1,0:T(8,128)(2,1)} %param.8) | copy-start | bytes 7864324
  26.7 14.5 %all-to-all-start.1 = ((bf16[2,32,256]{2,0,1:T(2,128)(2,1)}), bf16[2,32,256]{2,0,1:T(2,128)(2,1)S(1)}, u32[]{:S(2)}, u32[]{:S(2)}) async-start(bf16[2,32,256]{2,0,1:T(2,128)(2,1)} %bitcast.8), calls=%async_computation.1 | async-start | bytes 65536 | tf_op jit(solution)/shard_map/all_to_all | solution.py:95
  34.0 61.1 %all-gather.2.cloned.1.call-start = ((), (), s32[]{:S(2)}) async-start(), calls=%async_computation.2 | async-start | bytes 7864320 | tf_op jit(solution)/shard_map/all_gather | solution.py:125
  41.2 20.4 %all-to-all-start = ((bf16[32,32,256]{2,0,1:T(8,128)(2,1)}), bf16[32,32,256]{2,0,1:T(8,128)(2,1)S(1)}, u32[]{:S(2)}, u32[]{:S(2)}) async-start(bf16[32,32,256]{2,0,1:T(8,128)(2,1)} %copy.31), calls=%async_computation | async-start | bytes 1048576 | tf_op jit(solution)/shard_map/all_to_all | solution.py:88
  95.2 4.0 %copy-start = (bf16[64,16,2560]{2,0,1:T(8,128)(2,1)S(1)}, bf16[64,16,2560]{2,0,1:T(8,128)(2,1)}, u32[]{:S(2)}) copy-start(bf16[64,16,2560]{2,0,1:T(8,128)(2,1)} %all-gather.2.cloned.1.call-done) | copy-start | bytes 15728644
Sparse Core Ops, SparseCore 0:
  37.2 16.4 all-gather.1
where the time goes:
time: 111 us; the launch traced here: 110 us
  matrix products  30 us (27%)
  waiting for transfers between devices  18.8 us (17%)
  local copies, waits for them, and re-layouts  16.9 us (15%)
  other arithmetic  14.6 us (13%)
  between operations  13.7 us (12%)
  starting transfers between devices  10.9 us (10%)
  loops' own time  3 us (3%)
  blocking collectives  1.99 us (2%)
    all_to_all x1, waiting for transfers between devices, shards(): lax.all_to_all(ens_send.reshape(own_members, device_total, device_slots),...  16.5 us
    dot_general x1, matrix products, shards(): jnp.einsum('kmscq,jnscq->cmknj', weighted, trial_perturbation, precision=...  15 us
    dot_general x4, matrix products, fill_group(): jnp.dot(payload, picks, preferred_element_type=jnp.float32)  7.3 us
    all_to_all x1, starting transfers between devices, shards(): lax.all_to_all(meta_send.reshape(2, device_total, device_slots), ('member...  7.3 us
    unnamed x7, local copies, waits for them, and re-layouts  3.64 us
    reduce_sum x1, other arithmetic, shards(): state_sum = jnp.sum(state_block.astype(jnp.float32), axis=0)  3.58 us
    all_to_all x1, starting transfers between devices, shards(): lax.all_to_all(ens_send.reshape(own_members, device_total, device_slots),...  3.57 us
    sub x1, other arithmetic, shards(): trial_perturbation = background_trials - measured_average[None, None]  3.48 us
  transfers between devices with their start and end apart: 3, of which 2 were waited for; matrix products, arithmetic and copies ran while one was open for 33% of the time, Pallas kernels for 0%

commit v1 on v0

v1 whole, which is shorter than its diff:
```python
import functools

import jax
import jax.numpy as jnp
from jax import lax
from jax.experimental import pallas as pl
from jax.experimental.pallas import tpu as pltpu
from jax.sharding import PartitionSpec as P

NS_ITERS = 4
CAP = 32
PAIR = 2
GROUPS = CAP // PAIR
MESH = pl.DeviceIdType.MESH
F32 = jnp.float32
BF16 = jnp.bfloat16


def iota(shape, axis):
    return lax.broadcasted_iota(jnp.int32, shape, axis)


def dot(a, b, dims=((1,), (0,))):
    return lax.dot_general(a, b, (dims, ((), ())), preferred_element_type=F32)


def split(a):
    high = a.astype(BF16)
    return high, (a - high.astype(F32)).astype(BF16)


def dot3(a, b):
    (ah, al), (bh, bl) = a, b
    return dot(ah, bh) + (dot(ah, bl) + dot(al, bh))


def weights_kernel(
    spaces, ens, value, weight, region, order, rowkey, background,
    wall, other_background,
    ens_other, spread, packed, arrived, wide, own_weights, other_weights,
    pair_send, pair_recv, route_send, route_recv,
):
    own, count = ens.shape
    members = 2 * own
    regions = order.shape[0] // spaces
    rows = regions * PAIR
    main = GROUPS * members
    m = lax.axis_index("member")
    me = lax.axis_index("space")
    partner = {"member": 1 - m}

    barrier = pltpu.get_barrier_semaphore()
    pl.semaphore_signal(barrier, inc=1, device_id=partner, device_id_type=MESH)

    def greet(step, carry):
        pl.semaphore_signal(
            barrier, inc=1, device_id={"space": lax.rem(me + step, spaces)}, device_id_type=MESH
        )
        return carry

    lax.fori_loop(1, spaces, greet, 0)
    pl.semaphore_wait(barrier, spaces)

    def pair_copy(src, dst, index):
        return pltpu.make_async_remote_copy(
            src_ref=src, dst_ref=dst, send_sem=pair_send.at[index], recv_sem=pair_recv.at[index],
            device_id=partner, device_id_type=MESH,
        )

    ens_copy = pair_copy(ens, ens_other, 0)
    ens_copy.start()
    state_copy = pair_copy(background, other_background, 1)
    state_copy.start()

    block = 256
    upper = jnp.where(iota((block, block), 0) < iota((block, block), 1), 1.0, 0.0).astype(BF16)
    offset = jnp.zeros((order.shape[0], 1), F32)
    ranks = []
    for at in range(0, count, block):
        hit = jnp.where(order[...] == region[:, at : at + block], 1.0, 0.0)
        earlier = dot(hit.astype(BF16), upper) + offset
        ranks.append(jnp.sum(hit * earlier, axis=0, keepdims=True))
        offset = offset + jnp.sum(hit, axis=1, keepdims=True)
    rank = jnp.concatenate(ranks, axis=1).astype(jnp.int32)
    group = rank // PAIR
    key = region[...] * PAIR + rank % PAIR
    picks = jnp.where(rowkey[...] == key, 1.0, 0.0).astype(BF16)

    ens_copy.wait()
    here, there = ens[...].astype(F32), ens_other[...].astype(F32)
    mean = (jnp.sum(here, axis=0, keepdims=True) + jnp.sum(there, axis=0, keepdims=True)) / members
    root = jnp.sqrt(weight[...].astype(F32))
    here = ((here - mean) * root).astype(BF16)
    there = ((there - mean) * root).astype(BF16)
    departure = (value[...].astype(F32) - mean) * root
    for g in range(GROUPS):
        mask = jnp.where(group == g, 1.0, 0.0).astype(BF16)
        spread[pl.ds(pl.multiple_of(g * members + m * own, own), own), :] = here * mask
        spread[pl.ds(pl.multiple_of(g * members + (1 - m) * own, own), own), :] = there * mask
    spread[main:, :] = jnp.where(iota((128, count), 0) == group, departure, 0.0).astype(BF16)
    packed[...] = dot(picks, spread[...], ((1,), (1,))).astype(BF16)

    def place(index):
        return pl.ds(pl.multiple_of(index * rows, rows), rows)

    def route(dest, source, landing):
        return pltpu.make_async_remote_copy(
            src_ref=packed.at[place(dest)], dst_ref=arrived.at[place(landing)],
            send_sem=route_send.at[dest], recv_sem=route_recv.at[source],
            device_id={"space": dest}, device_id_type=MESH,
        )

    def send(step, carry):
        route(lax.rem(me + step, spaces), me, me).start()
        return carry

    def receive(step, carry):
        source = lax.rem(me + spaces - step, spaces)
        route(lax.rem(me + step, spaces), source, source).wait()
        return carry

    lax.fori_loop(1, spaces, send, 0)
    arrived[place(me), :] = packed[place(me), :]
    lax.fori_loop(1, spaces, receive, 0)
    for j in range(wide.shape[0]):
        wide[j] = arrived[:, j * 128 : (j + 1) * 128].astype(F32)

    eye = jnp.where(iota((members, members), 0) == iota((members, members), 1), 1.0, 0.0)
    lane = iota((spaces, 128), 1)
    fold = (iota((128, 2 * members), 0) % 2 == 0) == (iota((128, 2 * members), 1) < members)
    systems, projections, norms = [], [], []
    for r in range(regions):
        at = [pl.ds(r * PAIR + k, spaces, stride=rows) for k in range(PAIR)]
        extra = [wide[GROUPS // 2, a, :] for a in at]
        left, right = [], []
        for j in range(GROUPS // 2):
            for k in range(PAIR):
                left.append(wide[j, at[k], :])
                right.append(jnp.where(lane // 2 == j, extra[k], 0.0))
        anomalies = jnp.concatenate(left, axis=0).astype(BF16)
        departures = jnp.concatenate(right, axis=0).astype(BF16)
        gram = dot(anomalies, anomalies, ((0,), (0,)))
        product = dot(departures, anomalies, ((0,), (0,)))
        product = jnp.sum(jnp.where(fold, product, 0.0), axis=0, keepdims=True)
        projections.append(product[:, :members] + product[:, members:])
        system = (members - 1.0) * eye + (gram[:members, :members] + gram[members:, members:])
        norm = jnp.sum(jnp.sum(system * system, axis=0, keepdims=True), axis=1, keepdims=True)
        norm = jnp.sqrt(norm)
        norms.append(norm)
        systems.append(system / norm)

    direct = systems
    direct_parts = [split(a) for a in direct]
    correction = [1.5 * eye - 0.5 * a for a in direct]
    inverse = correction
    inverse_parts = [split(a) for a in inverse]
    direct = [dot3(a, c) for a, c in zip(direct_parts, inverse_parts)]
    for iteration in range(1, NS_ITERS):
        direct_parts = [split(a) for a in direct]
        correction = [1.5 * eye - 0.5 * dot3(b, a) for a, b in zip(direct_parts, inverse_parts)]
        correction_parts = [split(a) for a in correction]
        inverse = [dot3(c, b) for c, b in zip(correction_parts, inverse_parts)]
        if iteration < NS_ITERS - 1:
            direct = [dot3(a, c) for a, c in zip(direct_parts, correction_parts)]
            inverse_parts = [split(a) for a in inverse]

    for r in range(regions):
        root_part, norm = inverse[r], norms[r]
        inner = jnp.sum(root_part * projections[r], axis=1, keepdims=True)
        shift = jnp.sum(root_part * inner, axis=0, keepdims=True) / norm
        own_weights[r] = (jnp.sqrt((members - 1.0) / norm) * root_part + shift).astype(BF16)

    mine = pl.ds(pl.multiple_of(m * own, own), own)
    theirs = pl.ds(pl.multiple_of((1 - m) * own, own), own)
    weight_copy = pair_copy(own_weights.at[:, theirs, :], other_weights, 2)
    weight_copy.start()
    wall[m] = own_weights[:, mine, :]
    weight_copy.wait()
    wall[1 - m] = other_weights[...]
    state_copy.wait()


def analysis_kernel(weights, here, there, out, wide, retained):
    own, regions, tile = here.shape
    members = 2 * own
    half = own * regions
    m = lax.axis_index("member")

    @pl.when(pl.program_id(0) == 0)
    def expand():
        row, col = iota((half, half), 0), iota((half, half), 1)
        order = jnp.where(col == (row % regions) * own + row // regions, 1.0, 0.0).astype(BF16)
        columns = dot(order, weights[...])
        retained[...] = 1.0 - jnp.sum(columns, axis=1, keepdims=True)
        i, c = iota((members, 2 * half), 0), iota((members, 2 * half), 1)
        copies = jnp.where((c // regions + m * own) % members == i, 1.0, 0.0).astype(BF16)
        full = dot(columns.astype(BF16), copies)
        row, col = iota((half, 2 * half), 0), iota((half, 2 * half), 1)
        wide[:half] = jnp.where(row % regions == col % regions, full, 0.0).astype(BF16)
        row, col = iota((regions, 2 * half), 0), iota((regions, 2 * half), 1)
        wide[half:] = jnp.where(row == col % regions, 1.0 / members, 0.0).astype(BF16)

    total = dot(wide[:, :half], here[...].reshape(half, tile))
    total += dot(wide[:, half:], there[...].reshape(half, tile))
    state_mean = total[half:]
    combined = total[:half].reshape(own, regions, tile)
    share = retained[...].reshape(own, regions, 1)
    out[...] = (combined + share * state_mean[None]).astype(BF16)


def shards(spaces, background, obs_ens, obs_value, obs_weight, obs_region, region_order):
    own, own_regions, width = background.shape
    count = obs_ens.shape[1]
    regions = own_regions // 2
    members = 2 * own
    m = lax.axis_index("member")
    order = region_order.reshape(spaces, 2, regions)
    order = jnp.where(m == 0, order[:, 0], order[:, 1]).reshape(spaces * regions, 1)
    rowkey = (order * PAIR + jnp.arange(PAIR, dtype=jnp.int32)[None]).reshape(-1, 1)
    rows = regions * PAIR
    lanes = GROUPS * members + 128
    vmem = pl.BlockSpec(memory_space=pltpu.VMEM)
    hbm = pl.BlockSpec(memory_space=pl.ANY)
    weights, other = pl.pallas_call(
        functools.partial(weights_kernel, spaces),
        out_shape=(
            jax.ShapeDtypeStruct((2, regions, own, members), BF16),
            jax.ShapeDtypeStruct(background.shape, BF16),
        ),
        in_specs=[vmem] * 6 + [hbm],
        out_specs=(vmem, hbm),
        scratch_shapes=[
            pltpu.VMEM((own, count), BF16),
            pltpu.VMEM((lanes, count), BF16),
            pltpu.VMEM((spaces * rows, lanes), BF16),
            pltpu.VMEM((spaces * rows, lanes), BF16),
            pltpu.VMEM((lanes // 128, spaces * rows, 128), F32),
            pltpu.VMEM((regions, members, members), BF16),
            pltpu.VMEM((regions, own, members), BF16),
            pltpu.SemaphoreType.DMA((3,)),
            pltpu.SemaphoreType.DMA((3,)),
            pltpu.SemaphoreType.DMA((spaces,)),
            pltpu.SemaphoreType.DMA((spaces,)),
        ],
        compiler_params=pltpu.CompilerParams(
            collective_id=0, has_side_effects=True, vmem_limit_bytes=56 * 2**20
        ),
        name="region_weights",
    )(
        obs_ens, obs_value.reshape(1, count), obs_weight.reshape(1, count),
        obs_region.reshape(1, count), order, rowkey, background,
    )
    tile = 512
    half = own * own_regions
    block = pl.BlockSpec((own, own_regions, tile), lambda f: (0, 0, f))
    return pl.pallas_call(
        analysis_kernel,
        out_shape=jax.ShapeDtypeStruct(background.shape, BF16),
        grid=(width // tile,),
        in_specs=[pl.BlockSpec((half, members), lambda f: (0, 0)), block, block],
        out_specs=block,
        scratch_shapes=[
            pltpu.VMEM((half + own_regions, 2 * half), BF16),
            pltpu.VMEM((half, 1), F32),
        ],
        compiler_params=pltpu.CompilerParams(vmem_limit_bytes=40 * 2**20),
        name="analysis",
    )(weights.reshape(half, members), background, other)


def solution(mesh):
    return jax.shard_map(
        functools.partial(shards, mesh.shape["space"]),
        mesh=mesh,
        in_specs=(
            P("member", "space", None),
            P("member", "space"),
            P("space"),
            P("space"),
            P("space"),
            P(),
        ),
        out_specs=P("member", "space", None),
        check_vma=False,
    )
```

time: 111 us -> 44.6 us (0.40)
  the two profiles are of different devices: /device:TPU:0 before, /device:TPU:13 now
where the time goes in v1:
time: 44.6 us; the launch traced here: 44.3 us
  Pallas kernels  34 us (76%)
  local copies, waits for them, and re-layouts  9.45 us (21%)
  other arithmetic  0.78 us (2%)
    pallas_call x1, Pallas kernels, shards(): pl.pallas_call(functools.partial(weights_kernel, spaces), out_shape=(jax....  27.5 us
    pallas_call x1, Pallas kernels, shards(): pl.pallas_call(analysis_kernel, out_shape=jax.ShapeDtypeStruct(background...  6.54 us
    unnamed x6, local copies, waits for them, and re-layouts  2.64 us
    reshape x1, local copies, waits for them, and re-layouts, shards(): obs_value.reshape(1, count)  1.43 us
    reshape x1, local copies, waits for them, and re-layouts, shards(): obs_region.reshape(1, count)  1.3 us
    reshape x1, local copies, waits for them, and re-layouts, shards(): obs_weight.reshape(1, count)  1.28 us
    select_n x2, local copies, waits for them, and re-layouts, shards(): jnp.where(m == 0, order[:, 0], order[:, 1]).reshape(spaces * regions, 1)  1.21 us

profile of v1, /device:TPU:13, one launch (start us, length us, event | category | flops | bytes accessed | tf_op | source)
XLA Modules:
  0.0 44.3 jit_solution(16718681869686984662)
XLA Ops:
  0.0 0.0 copy-start
  0.0 1.4 %reshape.73.value = bf16[1,1280]{1,0:T(2,128)(2,1)} reshape(bf16[1280]{0:T(1024)(128)(2,1)} %param.8) | data formatting | bytes 5120 | tf_op jit(solution)/shard_map/reshape | solution.py:250
  1.4 1.3 %reshape.74.weight = bf16[1,1280]{1,0:T(2,128)(2,1)} reshape(bf16[1280]{0:T(1024)(128)(2,1)} %param.9) | data formatting | bytes 5120 | tf_op jit(solution)/shard_map/reshape | solution.py:250
  2.7 1.3 %reshape.75.region = s32[1,1280]{1,0:T(1,128)} reshape(s32[1280]{0:T(1024)} %param.10) | data formatting | bytes 10240 | tf_op jit(solution)/shard_map/reshape | solution.py:251
  4.0 0.8 %reshape.76 = s32[16,2,8]{2,1,0:T(2,128)S(1)} reshape(s32[256]{0:T(256)} %param.11) | data formatting | bytes 2048 | tf_op jit(solution)/shard_map/reshape | solution.py:217
  4.8 0.5 %broadcast.32 = s32[]{:T(128)} broadcast(s32[]{:T(128)} %constant.8.clone.1), dimensions={} | broadcast | bytes 8 | tf_op jit(solution)/shard_map/jit(_where)/select_n | solution.py:218
  5.3 0.7 %multiply_reduce_fusion = (s32[16,8]{1,0:T(8,128)S(1)}, s32[16,8]{1,0:T(8,128)S(1)}) fusion(s32[]{:T(128)} %broadcast.32, s32[16,2,8]{2,1,0:T(2,128)S(1)} %reshape.76, pred[]{:T(512)S(6)} %eq.3), kind=kLoop, calls=%fused_computation.2 | loop fusion | flops 256 | bytes 2053 | tf_op jit(solution)/shard_map/mul | solution.py:219
  6.0 0.1 mul.16
  6.1 0.1 iota_add_fusion
  6.2 0.7 %add.27.rowkey = s32[256,1]{1,0:T(8,128)} reshape(s32[128,2]{1,0:T(8,128)S(1)} %iota_add_fusion) | data formatting | bytes 2048 | tf_op jit(solution)/shard_map/add | solution.py:219
  6.9 0.7 %select_n.26.order = s32[128,1]{1,0:T(8,128)} reshape(s32[16,8]{1,0:T(8,128)S(1)} %get-tuple-element.10) | data formatting | bytes 1024 | tf_op jit(solution)/shard_map/jit(_where)/select_n | solution.py:218
  7.6 27.5 %region_weights.1 = (bf16[2,8,32,64]{3,2,1,0:T(8,128)(2,1)}, bf16[32,16,2560]{2,1,0:T(8,128)(2,1)}) custom-call(bf16[32,1280]{1,0:T(8,128)(2,1)} %ens.1, bf16[1,1280]{1,0:T(2,128)(2,1)} %reshape.73.value, bf16[1,1280]{1,0:T(2,128)(2,1)} %reshape.74.weight, s32[1,1280]{1,0:T(1,128)} %reshape.75.region, s32[128,1]{1,0:T(8,128)} %select_n.26.order, ...), custom_call_target="tpu_custom_call" | custom-call | tf_op jit(solution)/shard_map/region_weights/pallas_call | solution.py:224
  35.1 0.0 copy-done
  35.1 0.0 copy-start.1
  35.1 1.7 %copy-done.1 = bf16[32,16,2560]{2,1,0:T(8,128)(2,1)S(1)} copy-done((bf16[32,16,2560]{2,1,0:T(8,128)(2,1)S(1)}, bf16[32,16,2560]{2,1,0:T(8,128)(2,1)}, u32[]{:S(2)}) %copy-start.1) | copy-done | bytes 2621464
  36.9 0.0 copy-start.2
  36.9 0.9 %copy-done.2 = bf16[2,8,32,64]{3,2,1,0:T(8,128)(2,1)S(1)} copy-done((bf16[2,8,32,64]{3,2,1,0:T(8,128)(2,1)S(1)}, bf16[2,8,32,64]{3,2,1,0:T(8,128)(2,1)}, u32[]{:S(2)}) %copy-start.2) | copy-done | bytes 65560
  37.8 6.5 %analysis.1 = bf16[32,16,2560]{2,1,0:T(8,128)(2,1)} custom-call(bf16[512,64]{1,0:T(8,128)(2,1)S(1)} %bitcast.1, bf16[32,16,2560]{2,1,0:T(8,128)(2,1)S(1)} %copy-done, bf16[32,16,2560]{2,1,0:T(8,128)(2,1)S(1)} %copy-done.1), custom_call_target="tpu_custom_call" | custom-call | tf_op jit(solution)/shard_map/analysis/pallas_call | solution.py:256
Async XLA Ops:
  0.0 35.1 %copy-start = (bf16[32,16,2560]{2,1,0:T(8,128)(2,1)S(1)}, bf16[32,16,2560]{2,1,0:T(8,128)(2,1)}, u32[]{:S(2)}) copy-start(bf16[32,16,2560]{2,1,0:T(8,128)(2,1)} %here.1) | copy-start | bytes 7864324
  35.1 1.7 %copy-start.1 = (bf16[32,16,2560]{2,1,0:T(8,128)(2,1)S(1)}, bf16[32,16,2560]{2,1,0:T(8,128)(2,1)}, u32[]{:S(2)}) copy-start(bf16[32,16,2560]{2,1,0:T(8,128)(2,1)} %get-tuple-element.8.there) | copy-start | bytes 7864324
  36.9 0.9 %copy-start.2 = (bf16[2,8,32,64]{3,2,1,0:T(8,128)(2,1)S(1)}, bf16[2,8,32,64]{3,2,1,0:T(8,128)(2,1)}, u32[]{:S(2)}) copy-start(bf16[2,8,32,64]{3,2,1,0:T(8,128)(2,1)} %get-tuple-element.7) | copy-start | bytes 196612

commit v2 on v1

--- a/solution.py
+++ b/solution.py
@@ -35,16 +35,16 @@
 
 
 def weights_kernel(
-    spaces, ens, value, weight, region, order, rowkey, background,
+    spaces, ens, value, weight, region, region_order, background,
     wall, other_background,
     ens_other, spread, packed, arrived, wide, own_weights, other_weights,
     pair_send, pair_recv, route_send, route_recv,
 ):
     own, count = ens.shape
     members = 2 * own
-    regions = order.shape[0] // spaces
+    total = region_order.shape[0]
+    regions = total // spaces // 2
     rows = regions * PAIR
-    main = GROUPS * members
     m = lax.axis_index("member")
     me = lax.axis_index("space")
     partner = {"member": 1 - m}
@@ -72,32 +72,47 @@
     state_copy = pair_copy(background, other_background, 1)
     state_copy.start()
 
+    def column(height, per_space, per_region):
+        row, col = iota((height, 1), 0), iota((1, total), 1)
+        at = row // per_space * (2 * regions) + m * regions + row % per_space // per_region
+        held = region_order[...].reshape(1, total).astype(F32)
+        picked = jnp.sum(jnp.where(col == at, held, 0.0), axis=1, keepdims=True)
+        return picked.astype(jnp.int32)
+
+    order = column(spaces * regions, regions, 1)
+    rowkey = column(spaces * rows, rows, PAIR) * PAIR + iota((spaces * rows, 1), 0) % PAIR
+    region_row = region[...].reshape(1, count)
+    root = jnp.sqrt(weight[...].reshape(1, count).astype(F32))
+
     block = 256
     upper = jnp.where(iota((block, block), 0) < iota((block, block), 1), 1.0, 0.0).astype(BF16)
-    offset = jnp.zeros((order.shape[0], 1), F32)
+    offset = jnp.zeros((spaces * regions, 1), F32)
     ranks = []
     for at in range(0, count, block):
-        hit = jnp.where(order[...] == region[:, at : at + block], 1.0, 0.0)
+        hit = jnp.where(order == region_row[:, at : at + block], 1.0, 0.0)
         earlier = dot(hit.astype(BF16), upper) + offset
         ranks.append(jnp.sum(hit * earlier, axis=0, keepdims=True))
         offset = offset + jnp.sum(hit, axis=1, keepdims=True)
     rank = jnp.concatenate(ranks, axis=1).astype(jnp.int32)
     group = rank // PAIR
-    key = region[...] * PAIR + rank % PAIR
-    picks = jnp.where(rowkey[...] == key, 1.0, 0.0).astype(BF16)
+    key = region_row * PAIR + rank % PAIR
+    picks = jnp.where(rowkey == key, 1.0, 0.0).astype(BF16)
 
     ens_copy.wait()
     here, there = ens[...].astype(F32), ens_other[...].astype(F32)
     mean = (jnp.sum(here, axis=0, keepdims=True) + jnp.sum(there, axis=0, keepdims=True)) / members
-    root = jnp.sqrt(weight[...].astype(F32))
-    here = ((here - mean) * root).astype(BF16)
-    there = ((there - mean) * root).astype(BF16)
-    departure = (value[...].astype(F32) - mean) * root
+    here = (here - mean) * root
+    there = (there - mean) * root
+    departure = (value[...].reshape(1, count).astype(F32) - mean) * root
+    last = jnp.where(m == 0, there[own - 1 :], here[own - 1 :])
+    lift = last / (jnp.sqrt(F32(members)) - 1.0)
+    final = iota((own, 1), 0) == own - 1
+    here = jnp.where(final & (m == 1), departure, here + lift).astype(BF16)
+    there = jnp.where(final & (m == 0), departure, there + lift).astype(BF16)
     for g in range(GROUPS):
         mask = jnp.where(group == g, 1.0, 0.0).astype(BF16)
         spread[pl.ds(pl.multiple_of(g * members + m * own, own), own), :] = here * mask
         spread[pl.ds(pl.multiple_of(g * members + (1 - m) * own, own), own), :] = there * mask
-    spread[main:, :] = jnp.where(iota((128, count), 0) == group, departure, 0.0).astype(BF16)
     packed[...] = dot(picks, spread[...], ((1,), (1,))).astype(BF16)
 
     def place(index):
@@ -126,24 +141,25 @@
         wide[j] = arrived[:, j * 128 : (j + 1) * 128].astype(F32)
 
     eye = jnp.where(iota((members, members), 0) == iota((members, members), 1), 1.0, 0.0)
-    lane = iota((spaces, 128), 1)
-    fold = (iota((128, 2 * members), 0) % 2 == 0) == (iota((128, 2 * members), 1) < members)
+    edge = jnp.sqrt(F32(members))
+    kept_row, kept_col = iota((1, members), 1) < members - 1, iota((members, 1), 0) < members - 1
+    mirror_row = jnp.where(kept_row, 1.0, 1.0 - edge)
+    mirror_col = jnp.where(kept_col, 1.0, 1.0 - edge)
+    scale = 1.0 / (members - edge)
     systems, projections, norms = [], [], []
     for r in range(regions):
         at = [pl.ds(r * PAIR + k, spaces, stride=rows) for k in range(PAIR)]
-        extra = [wide[GROUPS // 2, a, :] for a in at]
-        left, right = [], []
-        for j in range(GROUPS // 2):
-            for k in range(PAIR):
-                left.append(wide[j, at[k], :])
-                right.append(jnp.where(lane // 2 == j, extra[k], 0.0))
+        left = [wide[j, at[k], :] for j in range(GROUPS // 2) for k in range(PAIR)]
         anomalies = jnp.concatenate(left, axis=0).astype(BF16)
-        departures = jnp.concatenate(right, axis=0).astype(BF16)
         gram = dot(anomalies, anomalies, ((0,), (0,)))
-        product = dot(departures, anomalies, ((0,), (0,)))
-        product = jnp.sum(jnp.where(fold, product, 0.0), axis=0, keepdims=True)
-        projections.append(product[:, :members] + product[:, members:])
-        system = (members - 1.0) * eye + (gram[:members, :members] + gram[members:, members:])
+        gram = gram[:members, :members] + gram[members:, members:]
+        projection = jnp.where(kept_row, gram[members - 1 :], 0.0)
+        gram = jnp.where(kept_row & kept_col, gram, 0.0)
+        reflected = jnp.sum(projection, axis=1, keepdims=True) * scale
+        projections.append(projection - reflected * mirror_row)
+        gram = gram - mirror_col * (jnp.sum(gram, axis=0, keepdims=True) * scale)
+        gram = gram - (jnp.sum(gram, axis=1, keepdims=True) * scale) * mirror_row
+        system = (members - 1.0) * eye + gram
         norm = jnp.sum(jnp.sum(system * system, axis=0, keepdims=True), axis=1, keepdims=True)
         norm = jnp.sqrt(norm)
         norms.append(norm)
@@ -188,17 +204,19 @@
 
     @pl.when(pl.program_id(0) == 0)
     def expand():
-        row, col = iota((half, half), 0), iota((half, half), 1)
-        order = jnp.where(col == (row % regions) * own + row // regions, 1.0, 0.0).astype(BF16)
+        row = iota((half, 1), 0)
+        region = row % regions
+        order = jnp.where(iota((1, half), 1) == region * own + row // regions, 1.0, 0.0)
+        order = order.astype(BF16)
         columns = dot(order, weights[...])
         retained[...] = 1.0 - jnp.sum(columns, axis=1, keepdims=True)
-        i, c = iota((members, 2 * half), 0), iota((members, 2 * half), 1)
-        copies = jnp.where((c // regions + m * own) % members == i, 1.0, 0.0).astype(BF16)
+        c = iota((1, 2 * half), 1)
+        member, lane_region = (c // regions + m * own) % members, c % regions
+        copies = jnp.where(member == iota((members, 1), 0), 1.0, 0.0).astype(BF16)
         full = dot(columns.astype(BF16), copies)
-        row, col = iota((half, 2 * half), 0), iota((half, 2 * half), 1)
-        wide[:half] = jnp.where(row % regions == col % regions, full, 0.0).astype(BF16)
-        row, col = iota((regions, 2 * half), 0), iota((regions, 2 * half), 1)
-        wide[half:] = jnp.where(row == col % regions, 1.0 / members, 0.0).astype(BF16)
+        wide[:half] = jnp.where(region == lane_region, full, 0.0).astype(BF16)
+        same = iota((regions, 1), 0) == lane_region
+        wide[half:] = jnp.where(same, 1.0 / members, 0.0).astype(BF16)
 
     total = dot(wide[:, :half], here[...].reshape(half, tile))
     total += dot(wide[:, half:], there[...].reshape(half, tile))
@@ -213,12 +231,8 @@
     count = obs_ens.shape[1]
     regions = own_regions // 2
     members = 2 * own
-    m = lax.axis_index("member")
-    order = region_order.reshape(spaces, 2, regions)
-    order = jnp.where(m == 0, order[:, 0], order[:, 1]).reshape(spaces * regions, 1)
-    rowkey = (order * PAIR + jnp.arange(PAIR, dtype=jnp.int32)[None]).reshape(-1, 1)
     rows = regions * PAIR
-    lanes = GROUPS * members + 128
+    lanes = GROUPS * members
     vmem = pl.BlockSpec(memory_space=pltpu.VMEM)
     hbm = pl.BlockSpec(memory_space=pl.ANY)
     weights, other = pl.pallas_call(
@@ -227,7 +241,7 @@
             jax.ShapeDtypeStruct((2, regions, own, members), BF16),
             jax.ShapeDtypeStruct(background.shape, BF16),
         ),
-        in_specs=[vmem] * 6 + [hbm],
+        in_specs=[vmem] * 5 + [hbm],
         out_specs=(vmem, hbm),
         scratch_shapes=[
             pltpu.VMEM((own, count), BF16),
@@ -247,8 +261,7 @@
         ),
         name="region_weights",
     )(
-        obs_ens, obs_value.reshape(1, count), obs_weight.reshape(1, count),
-        obs_region.reshape(1, count), order, rowkey, background,
+        obs_ens, obs_value, obs_weight, obs_region, region_order, background,
     )
     tile = 512
     half = own * own_regions
@@ -263,7 +276,7 @@
             pltpu.VMEM((half + own_regions, 2 * half), BF16),
             pltpu.VMEM((half, 1), F32),
         ],
-        compiler_params=pltpu.CompilerParams(vmem_limit_bytes=40 * 2**20),
+        compiler_params=pltpu.CompilerParams(vmem_limit_bytes=60 * 2**20),
         name="analysis",
     )(weights.reshape(half, members), background, other)
 

time: 44.6 us -> 34.2 us (0.77)
  local copies, waits for them, and re-layouts: 9.45 us -> 0 us
  other arithmetic: 0.78 us -> 0 us
    reshape x4 -> x0, local copies, waits for them, and re-layouts: 4.78 us -> none  [the longest x1 1.43 us: shards(): obs_value.reshape(1, count)]
    unnamed x6 -> x0, local copies, waits for them, and re-layouts: 2.64 us -> none
    pallas_call x1, Pallas kernels: 27.5 us -> 25.6 us  [shards(): pl.pallas_call(functools.partial(weights_kernel, spaces), out_shape=(jax....]
    pallas_call x1, Pallas kernels: 6.54 us -> 8.38 us  [shards(): pl.pallas_call(analysis_kernel, out_shape=jax.ShapeDtypeStruct(background...]
    select_n x2 -> x0, local copies, waits for them, and re-layouts: 1.21 us -> none  [shards(): jnp.where(m == 0, order[:, 0], order[:, 1]).reshape(spaces * regions, 1)]
    add x1 -> x0, local copies, waits for them, and re-layouts: 0.74 us -> none  [shards(): order * PAIR + jnp.arange(PAIR, dtype=jnp.int32)[None]]
    mul x1 -> x0, other arithmetic: 0.7 us -> none  [shards(): order * PAIR + jnp.arange(PAIR, dtype=jnp.int32)[None]]
where the time goes in v2:
time: 34.2 us; the launch traced here: 33.9 us
  Pallas kernels  33.9 us (99%)
    pallas_call x1, Pallas kernels, shards(): pl.pallas_call(functools.partial(weights_kernel, spaces), out_shape=(jax....  25.6 us
    pallas_call x1, Pallas kernels, shards(): pl.pallas_call(analysis_kernel, out_shape=jax.ShapeDtypeStruct(background...  8.38 us

profile of v2, /device:TPU:13, one launch (start us, length us, event | category | flops | bytes accessed | tf_op | source)
XLA Modules:
  0.0 33.9 jit_solution(5227657084116663330)
XLA Ops:
  0.0 25.6 %region_weights.1 = (bf16[2,8,32,64]{3,2,1,0:T(8,128)(2,1)}, bf16[32,16,2560]{2,1,0:T(8,128)(2,1)}) custom-call(bf16[32,1280]{1,0:T(8,128)(2,1)} %ens.1, bf16[1280]{0:T(1024)(128)(2,1)} %value.1, bf16[1280]{0:T(1024)(128)(2,1)} %weight.1, s32[1280]{0:T(1024)} %region.1, s32[256]{0:T(256)} %region_order.1, bf16[32,16,2560]{2,1,0:T(8,128)(2,1)} %here.1), custom_call_target="tpu_custom_call" | custom-call | tf_op jit(solution)/shard_map/region_weights/pallas_call | solution.py:238
  25.6 8.4 %analysis.1 = bf16[32,16,2560]{2,1,0:T(8,128)(2,1)} custom-call(bf16[512,64]{1,0:T(8,128)(2,1)} %bitcast.1, bf16[32,16,2560]{2,1,0:T(8,128)(2,1)} %here.1, bf16[32,16,2560]{2,1,0:T(8,128)(2,1)} %get-tuple-element.8.there), custom_call_target="tpu_custom_call" | custom-call | tf_op jit(solution)/shard_map/analysis/pallas_call | solution.py:269

commit v3 on v2

--- a/solution.py
+++ b/solution.py
@@ -11,6 +11,8 @@
 CAP = 32
 PAIR = 2
 GROUPS = CAP // PAIR
+CHUNKS = 2
+TILE = 512
 MESH = pl.DeviceIdType.MESH
 F32 = jnp.float32
 BF16 = jnp.bfloat16
@@ -109,36 +111,42 @@
     final = iota((own, 1), 0) == own - 1
     here = jnp.where(final & (m == 1), departure, here + lift).astype(BF16)
     there = jnp.where(final & (m == 0), departure, there + lift).astype(BF16)
-    for g in range(GROUPS):
-        mask = jnp.where(group == g, 1.0, 0.0).astype(BF16)
-        spread[pl.ds(pl.multiple_of(g * members + m * own, own), own), :] = here * mask
-        spread[pl.ds(pl.multiple_of(g * members + (1 - m) * own, own), own), :] = there * mask
-    packed[...] = dot(picks, spread[...], ((1,), (1,))).astype(BF16)
-
     def place(index):
         return pl.ds(pl.multiple_of(index * rows, rows), rows)
 
-    def route(dest, source, landing):
+    def route(chunk, dest, source, landing):
         return pltpu.make_async_remote_copy(
-            src_ref=packed.at[place(dest)], dst_ref=arrived.at[place(landing)],
-            send_sem=route_send.at[dest], recv_sem=route_recv.at[source],
+            src_ref=packed.at[chunk, place(dest)], dst_ref=arrived.at[chunk, place(landing)],
+            send_sem=route_send.at[chunk, dest], recv_sem=route_recv.at[chunk, source],
             device_id={"space": dest}, device_id_type=MESH,
         )
 
-    def send(step, carry):
-        route(lax.rem(me + step, spaces), me, me).start()
-        return carry
-
-    def receive(step, carry):
-        source = lax.rem(me + spaces - step, spaces)
-        route(lax.rem(me + step, spaces), source, source).wait()
-        return carry
-
-    lax.fori_loop(1, spaces, send, 0)
-    arrived[place(me), :] = packed[place(me), :]
-    lax.fori_loop(1, spaces, receive, 0)
-    for j in range(wide.shape[0]):
-        wide[j] = arrived[:, j * 128 : (j + 1) * 128].astype(F32)
+    span = GROUPS // CHUNKS
+    for chunk in range(CHUNKS):
+        for g in range(span):
+            mask = jnp.where(group == chunk * span + g, 1.0, 0.0).astype(BF16)
+            spread[pl.ds(pl.multiple_of(g * members + m * own, own), own), :] = here * mask
+            spread[pl.ds(pl.multiple_of(g * members + (1 - m) * own, own), own), :] = there * mask
+        packed[chunk] = dot(picks, spread[...], ((1,), (1,))).astype(BF16)
+
+        def send(step, carry):
+            route(chunk, lax.rem(me + step, spaces), me, me).start()
+            return carry
+
+        lax.fori_loop(1, spaces, send, 0)
+
+    tiles = wide.shape[0] // CHUNKS
+    for chunk in range(CHUNKS):
+
+        def receive(step, carry):
+            source = lax.rem(me + spaces - step, spaces)
+            route(chunk, lax.rem(me + step, spaces), source, source).wait()
+            return carry
+
+        arrived[chunk, place(me), :] = packed[chunk, place(me), :]
+        lax.fori_loop(1, spaces, receive, 0)
+        for j in range(tiles):
+            wide[chunk * tiles + j] = arrived[chunk, :, j * 128 : (j + 1) * 128].astype(F32)
 
     eye = jnp.where(iota((members, members), 0) == iota((members, members), 1), 1.0, 0.0)
     edge = jnp.sqrt(F32(members))
@@ -196,34 +204,52 @@
     state_copy.wait()
 
 
-def analysis_kernel(weights, here, there, out, wide, retained):
-    own, regions, tile = here.shape
+def analysis_kernel(
+    weights, here_any, there_any, out_any, here, there, out, wide, retained, sems
+):
+    own, regions, width = here.shape
     members = 2 * own
     half = own * regions
+    tile = TILE
     m = lax.axis_index("member")
-
-    @pl.when(pl.program_id(0) == 0)
-    def expand():
-        row = iota((half, 1), 0)
-        region = row % regions
-        order = jnp.where(iota((1, half), 1) == region * own + row // regions, 1.0, 0.0)
-        order = order.astype(BF16)
-        columns = dot(order, weights[...])
-        retained[...] = 1.0 - jnp.sum(columns, axis=1, keepdims=True)
-        c = iota((1, 2 * half), 1)
-        member, lane_region = (c // regions + m * own) % members, c % regions
-        copies = jnp.where(member == iota((members, 1), 0), 1.0, 0.0).astype(BF16)
-        full = dot(columns.astype(BF16), copies)
-        wide[:half] = jnp.where(region == lane_region, full, 0.0).astype(BF16)
-        same = iota((regions, 1), 0) == lane_region
-        wide[half:] = jnp.where(same, 1.0 / members, 0.0).astype(BF16)
-
-    total = dot(wide[:, :half], here[...].reshape(half, tile))
-    total += dot(wide[:, half:], there[...].reshape(half, tile))
-    state_mean = total[half:]
-    combined = total[:half].reshape(own, regions, tile)
-    share = retained[...].reshape(own, regions, 1)
-    out[...] = (combined + share * state_mean[None]).astype(BF16)
+    steps = [pl.ds(at, tile) for at in range(0, width, tile)]
+
+    def copy(kind, index):
+        source, target = ((here_any, here), (there_any, there), (out, out_any))[kind]
+        cut = steps[index]
+        return pltpu.make_async_copy(
+            source.at[:, :, cut], target.at[:, :, cut], sems.at[kind, index]
+        )
+
+    for index in range(len(steps)):
+        copy(0, index).start()
+        copy(1, index).start()
+
+    row = iota((half, 1), 0)
+    region = row % regions
+    order = jnp.where(iota((1, half), 1) == region * own + row // regions, 1.0, 0.0)
+    order = order.astype(BF16)
+    columns = dot(order, weights[...])
+    retained[...] = 1.0 - jnp.sum(columns, axis=1, keepdims=True)
+    c = iota((1, 2 * half), 1)
+    member, lane_region = (c // regions + m * own) % members, c % regions
+    copies = jnp.where(member == iota((members, 1), 0), 1.0, 0.0).astype(BF16)
+    full = dot(columns.astype(BF16), copies)
+    wide[:half] = jnp.where(region == lane_region, full, 0.0).astype(BF16)
+    same = iota((regions, 1), 0) == lane_region
+    wide[half:] = jnp.where(same, 1.0 / members, 0.0).astype(BF16)
+
+    for index, cut in enumerate(steps):
+        copy(0, index).wait()
+        copy(1, index).wait()
+        total = dot(wide[:, :half], here[:, :, cut].reshape(half, tile))
+        total += dot(wide[:, half:], there[:, :, cut].reshape(half, tile))
+        combined = total[:half].reshape(own, regions, tile)
+        share = retained[...].reshape(own, regions, 1)
+        out[:, :, cut] = (combined + share * total[half:][None]).astype(BF16)
+        copy(2, index).start()
+    for index in range(len(steps)):
+        copy(2, index).wait()
 
 
 def shards(spaces, background, obs_ens, obs_value, obs_weight, obs_region, region_order):
@@ -245,16 +271,16 @@
         out_specs=(vmem, hbm),
         scratch_shapes=[
             pltpu.VMEM((own, count), BF16),
-            pltpu.VMEM((lanes, count), BF16),
-            pltpu.VMEM((spaces * rows, lanes), BF16),
-            pltpu.VMEM((spaces * rows, lanes), BF16),
+            pltpu.VMEM((lanes // CHUNKS, count), BF16),
+            pltpu.VMEM((CHUNKS, spaces * rows, lanes // CHUNKS), BF16),
+            pltpu.VMEM((CHUNKS, spaces * rows, lanes // CHUNKS), BF16),
             pltpu.VMEM((lanes // 128, spaces * rows, 128), F32),
             pltpu.VMEM((regions, members, members), BF16),
             pltpu.VMEM((regions, own, members), BF16),
             pltpu.SemaphoreType.DMA((3,)),
             pltpu.SemaphoreType.DMA((3,)),
-            pltpu.SemaphoreType.DMA((spaces,)),
-            pltpu.SemaphoreType.DMA((spaces,)),
+            pltpu.SemaphoreType.DMA((CHUNKS, spaces)),
+            pltpu.SemaphoreType.DMA((CHUNKS, spaces)),
         ],
         compiler_params=pltpu.CompilerParams(
             collective_id=0, has_side_effects=True, vmem_limit_bytes=56 * 2**20
@@ -263,18 +289,19 @@
     )(
         obs_ens, obs_value, obs_weight, obs_region, region_order, background,
     )
-    tile = 512
     half = own * own_regions
-    block = pl.BlockSpec((own, own_regions, tile), lambda f: (0, 0, f))
     return pl.pallas_call(
         analysis_kernel,
         out_shape=jax.ShapeDtypeStruct(background.shape, BF16),
-        grid=(width // tile,),
-        in_specs=[pl.BlockSpec((half, members), lambda f: (0, 0)), block, block],
-        out_specs=block,
+        in_specs=[vmem, hbm, hbm],
+        out_specs=hbm,
         scratch_shapes=[
+            pltpu.VMEM(background.shape, BF16),
+            pltpu.VMEM(background.shape, BF16),
+            pltpu.VMEM(background.shape, BF16),
             pltpu.VMEM((half + own_regions, 2 * half), BF16),
             pltpu.VMEM((half, 1), F32),
+            pltpu.SemaphoreType.DMA((3, width // TILE)),
         ],
         compiler_params=pltpu.CompilerParams(vmem_limit_bytes=60 * 2**20),
         name="analysis",

time: 34.2 us -> 32.9 us (0.962)
  Pallas kernels: 33.9 us -> 32.7 us
    pallas_call x1, Pallas kernels: 8.38 us -> 7.44 us  [shards(): pl.pallas_call(analysis_kernel, out_shape=jax.ShapeDtypeStruct(background...]
where the time goes in v3:
time: 32.9 us; the launch traced here: 32.7 us
  Pallas kernels  32.7 us (99%)
    pallas_call x1, Pallas kernels, shards(): pl.pallas_call(functools.partial(weights_kernel, spaces), out_shape=(jax....  25.3 us
    pallas_call x1, Pallas kernels, shards(): pl.pallas_call(analysis_kernel, out_shape=jax.ShapeDtypeStruct(background...  7.44 us

profile of v3, /device:TPU:13, one launch (start us, length us, event | category | flops | bytes accessed | tf_op | source)
XLA Modules:
  0.0 32.7 jit_solution(4141484968299457790)
XLA Ops:
  0.0 25.3 %region_weights.1 = (bf16[2,8,32,64]{3,2,1,0:T(8,128)(2,1)}, bf16[32,16,2560]{2,1,0:T(8,128)(2,1)}) custom-call(bf16[32,1280]{1,0:T(8,128)(2,1)} %ens.1, bf16[1280]{0:T(1024)(128)(2,1)} %value.1, bf16[1280]{0:T(1024)(128)(2,1)} %weight.1, s32[1280]{0:T(1024)} %region.1, s32[256]{0:T(256)} %region_order.1, bf16[32,16,2560]{2,1,0:T(8,128)(2,1)} %here_any.1), custom_call_target="tpu_custom_call" | custom-call | tf_op jit(solution)/shard_map/region_weights/pallas_call | solution.py:264
  25.3 7.4 %analysis.1 = bf16[32,16,2560]{2,1,0:T(8,128)(2,1)} custom-call(bf16[512,64]{1,0:T(8,128)(2,1)} %bitcast.1, bf16[32,16,2560]{2,1,0:T(8,128)(2,1)} %here_any.1, bf16[32,16,2560]{2,1,0:T(8,128)(2,1)} %get-tuple-element.8.there_any), custom_call_target="tpu_custom_call" | custom-call | tf_op jit(solution)/shard_map/analysis/pallas_call | solution.py:293

commit v4 on v3

--- a/solution.py
+++ b/solution.py
@@ -61,19 +61,6 @@
         return carry
 
     lax.fori_loop(1, spaces, greet, 0)
-    pl.semaphore_wait(barrier, spaces)
-
-    def pair_copy(src, dst, index):
-        return pltpu.make_async_remote_copy(
-            src_ref=src, dst_ref=dst, send_sem=pair_send.at[index], recv_sem=pair_recv.at[index],
-            device_id=partner, device_id_type=MESH,
-        )
-
-    ens_copy = pair_copy(ens, ens_other, 0)
-    ens_copy.start()
-    state_copy = pair_copy(background, other_background, 1)
-    state_copy.start()
-
     def column(height, per_space, per_region):
         row, col = iota((height, 1), 0), iota((1, total), 1)
         at = row // per_space * (2 * regions) + m * regions + row % per_space // per_region
@@ -85,6 +72,19 @@
     rowkey = column(spaces * rows, rows, PAIR) * PAIR + iota((spaces * rows, 1), 0) % PAIR
     region_row = region[...].reshape(1, count)
     root = jnp.sqrt(weight[...].reshape(1, count).astype(F32))
+
+    pl.semaphore_wait(barrier, spaces)
+
+    def pair_copy(src, dst, index):
+        return pltpu.make_async_remote_copy(
+            src_ref=src, dst_ref=dst, send_sem=pair_send.at[index], recv_sem=pair_recv.at[index],
+            device_id=partner, device_id_type=MESH,
+        )
+
+    ens_copy = pair_copy(ens, ens_other, 0)
+    ens_copy.start()
+    state_copy = pair_copy(background, other_background, 1)
+    state_copy.start()
 
     block = 256
     upper = jnp.where(iota((block, block), 0) < iota((block, block), 1), 1.0, 0.0).astype(BF16)

time: 32.9 us -> 33.2 us (level)
  no operation moved by 1% of the time
where the time goes in v4:
time: 33.2 us; the launch traced here: 33 us
  Pallas kernels  33 us (99%)
    pallas_call x1, Pallas kernels, shards(): pl.pallas_call(functools.partial(weights_kernel, spaces), out_shape=(jax....  25.5 us
    pallas_call x1, Pallas kernels, shards(): pl.pallas_call(analysis_kernel, out_shape=jax.ShapeDtypeStruct(background...  7.44 us

profile of v4, /device:TPU:13, one launch (start us, length us, event | category | flops | bytes accessed | tf_op | source)
XLA Modules:
  0.0 33.0 jit_solution(5269609275454064)
XLA Ops:
  0.0 25.5 %region_weights.1 = (bf16[2,8,32,64]{3,2,1,0:T(8,128)(2,1)}, bf16[32,16,2560]{2,1,0:T(8,128)(2,1)}) custom-call(bf16[32,1280]{1,0:T(8,128)(2,1)} %ens.1, bf16[1280]{0:T(1024)(128)(2,1)} %value.1, bf16[1280]{0:T(1024)(128)(2,1)} %weight.1, s32[1280]{0:T(1024)} %region.1, s32[256]{0:T(256)} %region_order.1, bf16[32,16,2560]{2,1,0:T(8,128)(2,1)} %here_any.1), custom_call_target="tpu_custom_call" | custom-call | tf_op jit(solution)/shard_map/region_weights/pallas_call | solution.py:264
  25.5 7.4 %analysis.1 = bf16[32,16,2560]{2,1,0:T(8,128)(2,1)} custom-call(bf16[512,64]{1,0:T(8,128)(2,1)} %bitcast.1, bf16[32,16,2560]{2,1,0:T(8,128)(2,1)} %here_any.1, bf16[32,16,2560]{2,1,0:T(8,128)(2,1)} %get-tuple-element.8.there_any), custom_call_target="tpu_custom_call" | custom-call | tf_op jit(solution)/shard_map/analysis/pallas_call | solution.py:293
